TPU v7x, 32 devices: a whole 2x2x4 slice. The times are simulated.
32 devices in a mesh: blk: 16 (over z, y, core), uly: 2 (over x).
Axes of the slice: x: 2, y: 2, z: 4, core: 2. Of those that a mesh axis runs over, the one named last changes fastest.
Arguments:
- queries: bfloat16 [1024, 3072], P(('blk', 'uly')), may hold values from -40 to 40
- keys: bfloat16 [1024, 3072], P(('blk', 'uly')), may hold values from -6 to 6
- values: bfloat16 [1024, 3072], P(('blk', 'uly')), may hold values from -6 to 6
Outputs:
- attended: bfloat16 [1024, 3072], P(('blk', 'uly'))
All inputs are finite; a program needn't handle non-finite values.
Results may differ from a plain program's by a relative error of at most 0.0035.
Values may be sent and summed in bfloat16 or wider, within the bound.
No kernel may reach another device: no remote copies, remote signals or barrier semaphores. Data moves between devices by JAX's collectives and lax.ppermute only.
A program may use at most 128 MiB of HBM per device.

v0:
```python
import math

import jax
import jax.numpy as jnp
from jax import lax
from jax.sharding import PartitionSpec as P

HEADS = 24


def attend_block(running, query_heads, key_piece, value_piece):
    running_max, running_sum, weighted = running
    score_scale = 1.0 / math.sqrt(query_heads.shape[2])
    scores = (
        jnp.einsum("hre,phe->hrp", query_heads, key_piece, preferred_element_type=jnp.float32)
        * score_scale
    )
    new_max = jnp.maximum(running_max, jnp.max(scores, axis=-1))
    factor = jnp.exp(running_max - new_max)
    weights = jnp.exp(scores - new_max[..., None])
    running_sum = running_sum * factor + jnp.sum(weights, axis=-1)
    product = jnp.einsum(
        "hrp,phe->hre",
        weights.astype(jnp.bfloat16),
        value_piece,
        preferred_element_type=jnp.float32,
    )
    weighted = weighted * factor[..., None] + product
    return (new_max, running_sum, weighted)


def make_folder(query_heads, running, pieces):
    head_count = query_heads.shape[0]
    head_width = query_heads.shape[2]
    key_piece = pieces[0].reshape(-1, head_count, head_width)
    value_piece = pieces[1].reshape(-1, head_count, head_width)
    length = key_piece.shape[0]
    if length > 1024 and length % 1024 == 0:
        key_stack = key_piece.reshape(length // 1024, 1024, head_count, head_width)
        value_stack = value_piece.reshape(length // 1024, 1024, head_count, head_width)

        def advance(state_now, blocks):
            return (attend_block(state_now, query_heads, blocks[0], blocks[1]), None)

        running, unused = lax.scan(advance, running, (key_stack, value_stack))
        return running
    return attend_block(running, query_heads, key_piece, value_piece)


def start_state(query_heads):
    head_count, block_rows, head_width = query_heads.shape
    lowest = jnp.full((head_count, block_rows), -jnp.inf, jnp.float32)
    return (
        lowest,
        jnp.zeros((head_count, block_rows), jnp.float32),
        jnp.zeros((head_count, block_rows, head_width), jnp.float32),
    )


def finish(running_sum, weighted):
    head_count, block_rows, head_width = weighted.shape
    normed = weighted / running_sum[..., None]
    return (
        normed.transpose(1, 0, 2).reshape(block_rows, head_count * head_width).astype(jnp.bfloat16)
    )


def local(queries, keys, values):
    groups = lax.axis_size("uly")
    heads_here = HEADS // groups
    head_width = queries.shape[1] // HEADS
    query_rows, key_rows, value_rows = (
        lax.all_to_all(queries, "uly", split_axis=1, concat_axis=0, tiled=True),
        lax.all_to_all(keys, "uly", split_axis=1, concat_axis=0, tiled=True),
        lax.all_to_all(values, "uly", split_axis=1, concat_axis=0, tiled=True),
    )
    block_rows = query_rows.shape[0]
    query_heads = query_rows.reshape(block_rows, heads_here, head_width).transpose(1, 0, 2)
    final_max, final_sum, weighted = make_folder(
        query_heads,
        start_state(query_heads),
        (
            lax.all_gather(key_rows, "blk", axis=0, tiled=True),
            lax.all_gather(value_rows, "blk", axis=0, tiled=True),
        ),
    )
    local_out = finish(final_sum, weighted)
    return lax.all_to_all(local_out, "uly", split_axis=0, concat_axis=1, tiled=True)


def solution(mesh):
    in_specs = (P(("blk", "uly"), None), P(("blk", "uly"), None), P(("blk", "uly"), None))
    out_specs = P(("blk", "uly"), None)
    return jax.shard_map(local, mesh=mesh, in_specs=in_specs, out_specs=out_specs, check_vma=False)
```

profile of v0, /device:TPU:0, one launch (start us, length us, event | category | flops | bytes accessed | tf_op | source)
XLA Modules:
  0.0 132.0 jit_solution(8879187492064969567)
XLA Ops:
  6.5 0.0 all-gather.3.cloned.1.call-start
  6.5 0.9 copy.47
  7.5 9.0 %all_to_all.70 = bf16[32,2,1536]{2,0,1:T(8,128)(2,1)} all-to-all(bf16[32,2,1536]{2,0,1:T(8,128)(2,1)S(1)} %bitcast.51), channel_id=1, replica_groups=mesh['blk'=16,'uly'=2] {'uly'}, dimensions={1} | all-to-all | bytes 393216 | tf_op jit(solution)/shard_map/all_to_all | solution.py:74
  16.5 0.0 all-gather.3.cloned.1.call-update
  16.5 0.0 all-gather.5.cloned.1.call-start
  16.6 0.9 copy.46
  17.5 7.9 %all_to_all.71 = bf16[32,2,1536]{2,0,1:T(8,128)(2,1)} all-to-all(bf16[32,2,1536]{2,0,1:T(8,128)(2,1)S(1)} %bitcast.52), channel_id=1, replica_groups=mesh['blk'=16,'uly'=2] {'uly'}, dimensions={1} | all-to-all | bytes 393216 | tf_op jit(solution)/shard_map/all_to_all | solution.py:75
  25.4 0.0 all-gather.5.cloned.1.call-update
  25.4 1.0 copy.48
  26.4 7.2 %all_to_all.72 = bf16[32,2,1536]{2,0,1:T(8,128)(2,1)S(1)} all-to-all(bf16[32,2,1536]{2,0,1:T(8,128)(2,1)S(1)} %bitcast.53), channel_id=1, replica_groups=mesh['blk'=16,'uly'=2] {'uly'}, dimensions={1} | all-to-all | bytes 393216 | tf_op jit(solution)/shard_map/all_to_all | solution.py:73
  33.6 0.1 reshape.36
  33.7 28.8 %all-gather.3.cloned.1.call-done = bf16[1024,1536]{1,0:T(8,128)(2,1)} async-done(((bf16[64,1536]{1,0:T(8,128)(2,1)}), bf16[1024,1536]{1,0:T(8,128)(2,1)}) %all-gather.3.cloned.1.call-update) | async-done | bytes 3145744 | tf_op jit(solution)/shard_map/all_gather | solution.py:83
  62.5 4.7 %copy.24 = bf16[1024,1536]{0,1:T(8,128)(2,1)} copy(bf16[1024,1536]{1,0:T(8,128)(2,1)} %all-gather.3.cloned.1.call-done) | data formatting | bytes 6291456 | tf_op jit(solution)/shard_map/all_gather | solution.py:83
  67.2 2.7 %multiply_reduce_fusion = (f32[12,64]{1,0:T(8,128)S(1)}, f32[12,64,1024]{2,1,0:T(8,128)S(1)}) fusion(bf16[1024,12,128]{0,2,1:T(8,128)(2,1)} %bitcast.45, bf16[64,12,128]{2,1,0:T(8,128)(2,1)S(1)} %reshape.36), kind=kOutput, calls=%fused_computation.1 | convolution fusion | flops 202898688 | bytes 6491136 | tf_op jit(solution)/shard_map/hre,phe->hrp/dot_general | solution.py:15
  69.9 0.7 fusion
  70.6 38.2 %all-gather.5.cloned.1.call-done = bf16[1024,1536]{1,0:T(8,128)(2,1)} async-done(((bf16[64,1536]{1,0:T(8,128)(2,1)}), bf16[1024,1536]{1,0:T(8,128)(2,1)}) %all-gather.5.cloned.1.call-update) | async-done | bytes 3145744 | tf_op jit(solution)/shard_map/all_gather | solution.py:84
  108.8 4.7 %copy.27 = bf16[1024,1536]{0,1:T(8,128)(2,1)} copy(bf16[1024,1536]{1,0:T(8,128)(2,1)} %all-gather.5.cloned.1.call-done) | data formatting | bytes 6291456 | tf_op jit(solution)/shard_map/all_gather | solution.py:84
  113.5 3.2 %fusion.15 = bf16[64,12,128]{2,0,1:T(8,128)(2,1)S(1)} fusion(bf16[1024,12,128]{0,2,1:T(8,128)(2,1)} %bitcast.46, f32[12,64,1024]{2,1,0:T(8,128)S(1)} %get-tuple-element.6, f32[12,64]{1,0:T(8,128)S(1)} %get-tuple-element.5, f32[64,12]{0,1:T(8,128)S(1)} %bitcast_add_fusion, f32[64,12]{0,1:T(8,128)S(1)} %multiply_bitcast_fusion), kind=kOutput, calls=%fused_computation.10 | convolution fusion | flops 203980800 | bytes 6497280 | tf_op jit(solution)/shard_map/hrp,phe->hre/dot_general | solution.py:22
  116.7 0.1 copy.29
  116.8 0.1 convert_element_type.12
  117.0 7.5 %all_to_all.73 = bf16[2,32,1536]{2,1,0:T(8,128)(2,1)S(1)} all-to-all(bf16[2,32,1536]{2,1,0:T(8,128)(2,1)S(1)} %convert_element_type.12), channel_id=1, replica_groups=mesh['blk'=16,'uly'=2] {'uly'}, dimensions={0} | all-to-all | bytes 393216 | tf_op jit(solution)/shard_map/all_to_all | solution.py:88
  124.5 0.7 copy.36
  (2 shorter events, 0.0 us)
Async XLA Ops:
  6.5 56.0 %all-gather.3.cloned.1.call-start = ((), (), s32[]{:S(2)}) async-start(), calls=%async_computation.4 | async-start | bytes 3342336 | tf_op jit(solution)/shard_map/all_gather | solution.py:83
  16.5 92.3 %all-gather.5.cloned.1.call-start = ((), (), s32[]{:S(2)}) async-start(), calls=%async_computation.5 | async-start | bytes 3342336 | tf_op jit(solution)/shard_map/all_gather | solution.py:84
Sparse Core Ops, SparseCore 0:
  16.6 45.8 all-gather.2
  64.8 43.9 all-gather.4
where the time goes:
time: 133 us; the launch traced here: 132 us
  waiting for transfers between devices  67 us (50%)
  blocking collectives  31.6 us (24%)
  between operations  13.5 us (10%)
  local copies, waits for them, and re-layouts  13.3 us (10%)
  matrix products  5.83 us (4%)
    all_gather x1, waiting for transfers between devices, local(): lax.all_gather(value_rows, 'blk', axis=0, tiled=True)  38.2 us
    all_gather x1, waiting for transfers between devices, local(): lax.all_gather(key_rows, 'blk', axis=0, tiled=True)  28.8 us
    all_to_all x1, blocking collectives, local(): lax.all_to_all(keys, 'uly', split_axis=1, concat_axis=0, tiled=True)  9.01 us
    all_to_all x1, blocking collectives, local(): lax.all_to_all(values, 'uly', split_axis=1, concat_axis=0, tiled=True)  7.89 us
    all_to_all x1, blocking collectives, local(): lax.all_to_all(local_out, 'uly', split_axis=0, concat_axis=1, tiled=True)  7.54 us
    all_to_all x1, blocking collectives, local(): lax.all_to_all(queries, 'uly', split_axis=1, concat_axis=0, tiled=True)  7.21 us
    all_gather x1, local copies, waits for them, and re-layouts, local(): lax.all_gather(key_rows, 'blk', axis=0, tiled=True)  4.71 us
    all_gather x1, local copies, waits for them, and re-layouts, local(): lax.all_gather(value_rows, 'blk', axis=0, tiled=True)  4.67 us
  transfers between devices with their start and end apart: 2, of which 2 were waited for; matrix products, arithmetic and copies ran while one was open for 8% of the time, Pallas kernels for 0%

commit v1 on v0

--- a/solution.py
+++ b/solution.py
@@ -1,11 +1,16 @@
+import functools
 import math
 
 import jax
 import jax.numpy as jnp
 from jax import lax
+from jax.experimental import pallas as pl
+from jax.experimental.pallas import tpu as pltpu
 from jax.sharding import PartitionSpec as P
 
 HEADS = 24
+AXES = ("blk", "uly")
+QUERY_TILE = 256
 
 
 def attend_block(running, query_heads, key_piece, value_piece):
@@ -88,7 +93,47 @@
     return lax.all_to_all(local_out, "uly", split_axis=0, concat_axis=1, tiled=True)
 
 
+def head_kernel(tile, received, out):
+    devices, rows, width = out.shape
+    tokens = devices * rows
+    factor = math.log2(math.e) / math.sqrt(width)
+    key_rows = received[:, rows : 2 * rows, :].reshape(tokens, width)
+    value_rows = received[:, 2 * rows :, :].reshape(tokens, width)
+    step = tile // rows
+    for first in range(0, devices, step):
+        query_rows = received[first : first + step, :rows, :].reshape(tile, width)
+        scores = lax.dot_general(
+            query_rows, key_rows, (((1,), (1,)), ((), ())), preferred_element_type=jnp.float32
+        )
+        highest = jnp.max(scores, axis=1, keepdims=True)
+        weights = jnp.exp2((scores - highest) * factor)
+        denominator = jnp.sum(weights, axis=1, keepdims=True)
+        summed = jnp.dot(
+            weights.astype(jnp.bfloat16), value_rows, preferred_element_type=jnp.float32
+        )
+        attended = (summed / denominator).astype(jnp.bfloat16)
+        out[first : first + step] = attended.reshape(step, rows, width)
+
+
+def whole_heads(queries, keys, values):
+    devices = lax.axis_size(AXES)
+    rows, dim = queries.shape
+    width = dim // HEADS
+    packed = jnp.concatenate([queries, keys, values], axis=0).reshape(3 * rows, HEADS, width)
+    packed = jnp.pad(packed.transpose(1, 0, 2), ((0, devices - HEADS), (0, 0), (0, 0)))
+    received = lax.all_to_all(packed, AXES, split_axis=0, concat_axis=0, tiled=True)
+    attended = pl.pallas_call(
+        functools.partial(head_kernel, QUERY_TILE),
+        out_shape=jax.ShapeDtypeStruct((devices, rows, width), jnp.bfloat16),
+        compiler_params=pltpu.CompilerParams(vmem_limit_bytes=40 * 1024 * 1024),
+    )(received)
+    returned = lax.all_to_all(attended, AXES, split_axis=0, concat_axis=0, tiled=True)
+    return returned[:HEADS].transpose(1, 0, 2).reshape(rows, dim)
+
+
 def solution(mesh):
-    in_specs = (P(("blk", "uly"), None), P(("blk", "uly"), None), P(("blk", "uly"), None))
-    out_specs = P(("blk", "uly"), None)
-    return jax.shard_map(local, mesh=mesh, in_specs=in_specs, out_specs=out_specs, check_vma=False)
+    in_specs = (P(AXES, None), P(AXES, None), P(AXES, None))
+    out_specs = P(AXES, None)
+    devices = mesh.shape["blk"] * mesh.shape["uly"]
+    body = whole_heads if HEADS <= devices < 2 * HEADS else local
+    return jax.shard_map(body, mesh=mesh, in_specs=in_specs, out_specs=out_specs, check_vma=False)

time: 133 us -> 46 us (0.35)
  waiting for transfers between devices: 67 us -> 0 us
  between operations: 13.5 us -> 0.02 us
  local copies, waits for them, and re-layouts: 13.3 us -> 0.76 us
  blocking collectives: 31.6 us -> 41.8 us
  matrix products: 5.83 us -> 0 us
  Pallas kernels: 0 us -> 2.03 us
    all_gather x2 -> x0, waiting for transfers between devices: 67 us -> none  [the longest x1 38.2 us: local(): lax.all_gather(value_rows, 'blk', axis=0, tiled=True)]
    all_to_all x4 -> x2, blocking collectives: 31.6 us -> 41.8 us  [the longest x1 27.7 us: whole_heads(): lax.all_to_all(packed, AXES, split_axis=0, concat_axis=0, tiled=True)]
    all_gather x2 -> x0, local copies, waits for them, and re-layouts: 9.38 us -> none  [the longest x1 4.71 us: local(): lax.all_gather(key_rows, 'blk', axis=0, tiled=True)]
    dot_general x2 -> x0, matrix products: 5.83 us -> none  [the longest x1 3.16 us: attend_block(): jnp.einsum('hrp,phe->hre', weights.astype(jnp.bfloat16), value_piece, pre...]
    all_to_all x4 -> x0, local copies, waits for them, and re-layouts: 3.53 us -> none  [the longest x1 0.96 us: local(): lax.all_to_all(queries, 'uly', split_axis=1, concat_axis=0, tiled=True)]
    pallas_call x0 -> x1, Pallas kernels: none -> 2.03 us  [whole_heads(): pl.pallas_call(functools.partial(head_kernel, QUERY_TILE), out_shape=jax....]
  transfers between devices with their start and end apart: 2 -> 0, of which waited for: 2 -> 0; matrix products, arithmetic and copies ran while one was open for 8% -> 0% of each run, Pallas kernels for 0% -> 0%
where the time goes in v1:
time: 46 us; the launch traced here: 45.9 us
  blocking collectives  41.8 us (91%)
  Pallas kernels  2.03 us (4%)
  other arithmetic  1.22 us (3%)
  local copies, waits for them, and re-layouts  0.76 us (2%)
    all_to_all x1, blocking collectives, whole_heads(): lax.all_to_all(packed, AXES, split_axis=0, concat_axis=0, tiled=True)  27.7 us
    all_to_all x1, blocking collectives, whole_heads(): lax.all_to_all(attended, AXES, split_axis=0, concat_axis=0, tiled=True)  14.1 us
    pallas_call x1, Pallas kernels, whole_heads(): pl.pallas_call(functools.partial(head_kernel, QUERY_TILE), out_shape=jax....  2.03 us
    transpose x1, other arithmetic, whole_heads(): packed.transpose(1, 0, 2)  1.22 us

profile of v1, /device:TPU:0, one launch (start us, length us, event | category | flops | bytes accessed | tf_op | source)
XLA Modules:
  0.0 45.9 jit_solution(7612222191659311220)
XLA Ops:
  0.0 1.2 %bitcast_bitcast_fusion = bf16[24,96,128]{2,1,0:T(8,128)(2,1)S(1)} fusion(bf16[32,3072]{1,0:T(8,128)(2,1)} %param.5, bf16[32,3072]{1,0:T(8,128)(2,1)} %param.4, bf16[32,3072]{1,0:T(8,128)(2,1)} %param.3), kind=kLoop, calls=%fused_computation | loop fusion | flops 1769472 | bytes 1179648 | tf_op jit(solution)/shard_map/transpose | solution.py:123
  1.2 0.1 pad.4
  1.3 27.7 %all_to_all.10.received = bf16[32,96,128]{2,1,0:T(8,128)(2,1)S(1)} all-to-all(bf16[32,96,128]{2,1,0:T(8,128)(2,1)S(1)} %pad.4), channel_id=1, replica_groups=mesh['blk'=16,'uly'=2] {'blk','uly'}, dimensions={0} | all-to-all | bytes 1572864 | tf_op jit(solution)/shard_map/all_to_all | solution.py:124
  29.0 2.0 %shard_map.37 = bf16[32,32,128]{2,1,0:T(8,128)(2,1)S(1)} custom-call(bf16[32,96,128]{2,1,0:T(8,128)(2,1)S(1)} %all_to_all.10.received), custom_call_target="tpu_custom_call" | custom-call | tf_op jit(solution)/shard_map/pallas_call | solution.py:125
  31.1 14.1 %all_to_all.11 = bf16[32,32,128]{2,1,0:T(8,128)(2,1)S(1)} all-to-all(bf16[32,32,128]{2,1,0:T(8,128)(2,1)S(1)} %shard_map.37), channel_id=1, replica_groups=mesh['blk'=16,'uly'=2] {'blk','uly'}, dimensions={0} | all-to-all | bytes 524288 | tf_op jit(solution)/shard_map/all_to_all | solution.py:130
  45.2 0.7 %copy_bitcast_fusion = bf16[32,3072]{1,0:T(8,128)(2,1)} fusion(bf16[32,32,128]{2,1,0:T(8,128)(2,1)S(1)} %all_to_all.11), kind=kLoop, calls=%fused_computation.2 | loop fusion | bytes 393216 | tf_op jit(solution)/shard_map/reshape | solution.py:131

commit v2 on v1

--- a/solution.py
+++ b/solution.py
@@ -11,6 +11,7 @@
 HEADS = 24
 AXES = ("blk", "uly")
 QUERY_TILE = 256
+STRIDE = 3
 
 
 def attend_block(running, query_heads, key_piece, value_piece):
@@ -93,41 +94,62 @@
     return lax.all_to_all(local_out, "uly", split_axis=0, concat_axis=1, tiled=True)
 
 
-def head_kernel(tile, received, out):
+def participants(devices):
+    return [STRIDE * i % devices for i in range(devices)]
+
+
+def head_kernel(order, tile, received, out):
     devices, rows, width = out.shape
     tokens = devices * rows
     factor = math.log2(math.e) / math.sqrt(width)
-    key_rows = received[:, rows : 2 * rows, :].reshape(tokens, width)
-    value_rows = received[:, 2 * rows :, :].reshape(tokens, width)
     step = tile // rows
-    for first in range(0, devices, step):
+    me = lax.axis_index("blk") * lax.axis_size("uly") + lax.axis_index("uly")
+    idle = functools.reduce(jnp.logical_or, [me == device for device in order[HEADS:]], False)
+
+    def scores_of(first, key_rows):
         query_rows = received[first : first + step, :rows, :].reshape(tile, width)
-        scores = lax.dot_general(
+        return lax.dot_general(
             query_rows, key_rows, (((1,), (1,)), ((), ())), preferred_element_type=jnp.float32
         )
-        highest = jnp.max(scores, axis=1, keepdims=True)
-        weights = jnp.exp2((scores - highest) * factor)
-        denominator = jnp.sum(weights, axis=1, keepdims=True)
-        summed = jnp.dot(
-            weights.astype(jnp.bfloat16), value_rows, preferred_element_type=jnp.float32
-        )
-        attended = (summed / denominator).astype(jnp.bfloat16)
-        out[first : first + step] = attended.reshape(step, rows, width)
+
+    @pl.when(jnp.logical_not(idle))
+    def attend():
+        key_rows = received[:, rows : 2 * rows, :].reshape(tokens, width)
+        value_rows = received[:, 2 * rows :, :].reshape(tokens, width)
+        extended = jnp.concatenate([value_rows, jnp.ones_like(value_rows)], axis=1)
+        scores = scores_of(0, key_rows)
+        for first in range(0, devices, step):
+            after = first + step
+            later = scores_of(after, key_rows) if after < devices else None
+            highest = jnp.max(scores, axis=1, keepdims=True)
+            weights = jnp.exp2((scores - highest) * factor).astype(jnp.bfloat16)
+            summed = jnp.dot(weights, extended, preferred_element_type=jnp.float32)
+            attended = (summed[:, :width] / summed[:, width:]).astype(jnp.bfloat16)
+            out[first:after] = attended.reshape(step, rows, width)
+            scores = later
 
 
 def whole_heads(queries, keys, values):
     devices = lax.axis_size(AXES)
     rows, dim = queries.shape
     width = dim // HEADS
+    order = participants(devices)
+    exchange = functools.partial(
+        lax.all_to_all,
+        axis_name=AXES,
+        split_axis=0,
+        concat_axis=0,
+        axis_index_groups=[order],
+        tiled=True,
+    )
     packed = jnp.concatenate([queries, keys, values], axis=0).reshape(3 * rows, HEADS, width)
     packed = jnp.pad(packed.transpose(1, 0, 2), ((0, devices - HEADS), (0, 0), (0, 0)))
-    received = lax.all_to_all(packed, AXES, split_axis=0, concat_axis=0, tiled=True)
     attended = pl.pallas_call(
-        functools.partial(head_kernel, QUERY_TILE),
+        functools.partial(head_kernel, order, min(QUERY_TILE, devices * rows)),
         out_shape=jax.ShapeDtypeStruct((devices, rows, width), jnp.bfloat16),
         compiler_params=pltpu.CompilerParams(vmem_limit_bytes=40 * 1024 * 1024),
-    )(received)
-    returned = lax.all_to_all(attended, AXES, split_axis=0, concat_axis=0, tiled=True)
+    )(exchange(packed))
+    returned = exchange(attended)
     return returned[:HEADS].transpose(1, 0, 2).reshape(rows, dim)
 
 
@@ -135,5 +157,5 @@
     in_specs = (P(AXES, None), P(AXES, None), P(AXES, None))
     out_specs = P(AXES, None)
     devices = mesh.shape["blk"] * mesh.shape["uly"]
-    body = whole_heads if HEADS <= devices < 2 * HEADS else local
+    body = whole_heads if HEADS <= devices < 2 * HEADS and devices % STRIDE else local
     return jax.shard_map(body, mesh=mesh, in_specs=in_specs, out_specs=out_specs, check_vma=False)

time: 46 us -> 44 us (0.957)
  blocking collectives: 41.8 us -> 40.3 us
  Pallas kernels: 2.03 us -> 1.53 us
    all_to_all x2, blocking collectives: 41.8 us -> 40.3 us  [the longest x1 28.5 us: whole_heads(): exchange(packed)]
    pallas_call x1, Pallas kernels: 2.03 us -> 1.53 us  [whole_heads(): pl.pallas_call(functools.partial(head_kernel, order, min(QUERY_TILE, devi...]
where the time goes in v2:
time: 44 us; the launch traced here: 43.8 us
  blocking collectives  40.3 us (92%)
  Pallas kernels  1.53 us (3%)
  other arithmetic  1.22 us (3%)
  local copies, waits for them, and re-layouts  0.76 us (2%)
    all_to_all x1, blocking collectives, whole_heads(): exchange(packed)  28.5 us
    all_to_all x1, blocking collectives, whole_heads(): returned = exchange(attended)  11.7 us
    pallas_call x1, Pallas kernels, whole_heads(): pl.pallas_call(functools.partial(head_kernel, order, min(QUERY_TILE, devi...  1.53 us
    transpose x1, other arithmetic, whole_heads(): packed.transpose(1, 0, 2)  1.22 us

profile of v2, /device:TPU:0, one launch (start us, length us, event | category | flops | bytes accessed | tf_op | source)
XLA Modules:
  0.0 43.8 jit_solution(8384077656513710372)
XLA Ops:
  0.0 1.2 %bitcast_bitcast_fusion = bf16[24,96,128]{2,1,0:T(8,128)(2,1)S(1)} fusion(bf16[32,3072]{1,0:T(8,128)(2,1)} %param.5, bf16[32,3072]{1,0:T(8,128)(2,1)} %param.4, bf16[32,3072]{1,0:T(8,128)(2,1)} %param.3), kind=kLoop, calls=%fused_computation | loop fusion | flops 1769472 | bytes 1179648 | tf_op jit(solution)/shard_map/transpose | solution.py:146
  1.2 0.1 pad.4
  1.3 28.5 %all_to_all.10.received = bf16[32,96,128]{2,1,0:T(8,128)(2,1)S(1)} all-to-all(bf16[32,96,128]{2,1,0:T(8,128)(2,1)S(1)} %pad.4), channel_id=1, replica_groups={{0,3,6,9,12,15,18,21,24,27,30,1,4,7,10,13,16,19,22,25,28,31,2,5,8,11,14..., dimensions={0} | all-to-all | bytes 1572864 | tf_op jit(solution)/shard_map/all_to_all | solution.py:151
  29.8 1.5 %shard_map.37 = bf16[32,32,128]{2,1,0:T(8,128)(2,1)S(1)} custom-call(bf16[32,96,128]{2,1,0:T(8,128)(2,1)S(1)} %all_to_all.10.received), custom_call_target="tpu_custom_call" | custom-call | tf_op jit(solution)/shard_map/pallas_call | solution.py:147
  31.4 11.7 %all_to_all.11 = bf16[32,32,128]{2,1,0:T(8,128)(2,1)S(1)} all-to-all(bf16[32,32,128]{2,1,0:T(8,128)(2,1)S(1)} %shard_map.37), channel_id=1, replica_groups={{0,3,6,9,12,15,18,21,24,27,30,1,4,7,10,13,16,19,22,25,28,31,2,5,8,11,14..., dimensions={0} | all-to-all | bytes 524288 | tf_op jit(solution)/shard_map/all_to_all | solution.py:152
  43.1 0.7 %copy_bitcast_fusion = bf16[32,3072]{1,0:T(8,128)(2,1)} fusion(bf16[32,32,128]{2,1,0:T(8,128)(2,1)S(1)} %all_to_all.11), kind=kLoop, calls=%fused_computation.2 | loop fusion | bytes 393216 | tf_op jit(solution)/shard_map/reshape | solution.py:153

commit v3 on v2

--- a/solution.py
+++ b/solution.py
@@ -11,7 +11,8 @@
 HEADS = 24
 AXES = ("blk", "uly")
 QUERY_TILE = 256
-STRIDE = 3
+STRIDE = 11
+START = 19
 
 
 def attend_block(running, query_heads, key_piece, value_piece):
@@ -94,8 +95,16 @@
     return lax.all_to_all(local_out, "uly", split_axis=0, concat_axis=1, tiled=True)
 
 
-def participants(devices):
-    return [STRIDE * i % devices for i in range(devices)]
+def participants(blocks, groups):
+    devices = blocks * groups
+    if blocks % 4 or math.gcd(STRIDE, devices) > 1:
+        return list(range(devices))
+    order = []
+    for place in range(devices):
+        pair, rest = divmod((STRIDE * place + START) % devices, 2 * groups)
+        group, half = divmod(rest, 2)
+        order.append(((pair ^ 1) * 2 + (half ^ 1)) * groups + group)
+    return order
 
 
 def head_kernel(order, tile, received, out):
@@ -133,7 +142,7 @@
     devices = lax.axis_size(AXES)
     rows, dim = queries.shape
     width = dim // HEADS
-    order = participants(devices)
+    order = participants(lax.axis_size("blk"), lax.axis_size("uly"))
     exchange = functools.partial(
         lax.all_to_all,
         axis_name=AXES,
@@ -157,5 +166,5 @@
     in_specs = (P(AXES, None), P(AXES, None), P(AXES, None))
     out_specs = P(AXES, None)
     devices = mesh.shape["blk"] * mesh.shape["uly"]
-    body = whole_heads if HEADS <= devices < 2 * HEADS and devices % STRIDE else local
+    body = whole_heads if HEADS <= devices < 2 * HEADS else local
     return jax.shard_map(body, mesh=mesh, in_specs=in_specs, out_specs=out_specs, check_vma=False)

time: 44 us -> 43.6 us (level)
    all_to_all x1, blocking collectives: 28.5 us -> 27.7 us  [whole_heads(): exchange(packed)]
    all_to_all x1, blocking collectives: 11.7 us -> 12.2 us  [whole_heads(): returned = exchange(attended)]
where the time goes in v3:
time: 43.6 us; the launch traced here: 43.4 us
  blocking collectives  39.9 us (92%)
  Pallas kernels  1.52 us (3%)
  other arithmetic  1.22 us (3%)
  local copies, waits for them, and re-layouts  0.76 us (2%)
    all_to_all x1, blocking collectives, whole_heads(): exchange(packed)  27.7 us
    all_to_all x1, blocking collectives, whole_heads(): returned = exchange(attended)  12.2 us
    pallas_call x1, Pallas kernels, whole_heads(): pl.pallas_call(functools.partial(head_kernel, order, min(QUERY_TILE, devi...  1.52 us
    transpose x1, other arithmetic, whole_heads(): packed.transpose(1, 0, 2)  1.22 us

profile of v3, /device:TPU:0, one launch (start us, length us, event | category | flops | bytes accessed | tf_op | source)
XLA Modules:
  0.0 43.4 jit_solution(9230190440432314841)
XLA Ops:
  0.0 1.2 %bitcast_bitcast_fusion = bf16[24,96,128]{2,1,0:T(8,128)(2,1)S(1)} fusion(bf16[32,3072]{1,0:T(8,128)(2,1)} %param.5, bf16[32,3072]{1,0:T(8,128)(2,1)} %param.4, bf16[32,3072]{1,0:T(8,128)(2,1)} %param.3), kind=kLoop, calls=%fused_computation | loop fusion | flops 1769472 | bytes 1179648 | tf_op jit(solution)/shard_map/transpose | solution.py:155
  1.2 0.1 pad.4
  1.3 27.7 %all_to_all.10.received = bf16[32,96,128]{2,1,0:T(8,128)(2,1)S(1)} all-to-all(bf16[32,96,128]{2,1,0:T(8,128)(2,1)S(1)} %pad.4), channel_id=1, replica_groups={{21,27,12,18,25,15,16,6,13,19,4,10,17,7,8,30,5,11,28,2,9,31,0,22,29,3,2..., dimensions={0} | all-to-all | bytes 1572864 | tf_op jit(solution)/shard_map/all_to_all | solution.py:160
  29.0 1.5 %shard_map.37 = bf16[32,32,128]{2,1,0:T(8,128)(2,1)S(1)} custom-call(bf16[32,96,128]{2,1,0:T(8,128)(2,1)S(1)} %all_to_all.10.received), custom_call_target="tpu_custom_call" | custom-call | tf_op jit(solution)/shard_map/pallas_call | solution.py:156
  30.6 12.2 %all_to_all.11 = bf16[32,32,128]{2,1,0:T(8,128)(2,1)S(1)} all-to-all(bf16[32,32,128]{2,1,0:T(8,128)(2,1)S(1)} %shard_map.37), channel_id=1, replica_groups={{21,27,12,18,25,15,16,6,13,19,4,10,17,7,8,30,5,11,28,2,9,31,0,22,29,3,2..., dimensions={0} | all-to-all | bytes 524288 | tf_op jit(solution)/shard_map/all_to_all | solution.py:161
  42.7 0.7 %copy_bitcast_fusion = bf16[32,3072]{1,0:T(8,128)(2,1)} fusion(bf16[32,32,128]{2,1,0:T(8,128)(2,1)S(1)} %all_to_all.11), kind=kLoop, calls=%fused_computation.2 | loop fusion | bytes 393216 | tf_op jit(solution)/shard_map/reshape | solution.py:162

commit v4 on v3

--- a/solution.py
+++ b/solution.py
@@ -125,15 +125,17 @@
     def attend():
         key_rows = received[:, rows : 2 * rows, :].reshape(tokens, width)
         value_rows = received[:, 2 * rows :, :].reshape(tokens, width)
-        extended = jnp.concatenate([value_rows, jnp.ones_like(value_rows)], axis=1)
         scores = scores_of(0, key_rows)
         for first in range(0, devices, step):
             after = first + step
             later = scores_of(after, key_rows) if after < devices else None
             highest = jnp.max(scores, axis=1, keepdims=True)
-            weights = jnp.exp2((scores - highest) * factor).astype(jnp.bfloat16)
-            summed = jnp.dot(weights, extended, preferred_element_type=jnp.float32)
-            attended = (summed[:, :width] / summed[:, width:]).astype(jnp.bfloat16)
+            weights = jnp.exp2((scores - highest) * factor)
+            denominator = jnp.sum(weights, axis=1, keepdims=True)
+            summed = jnp.dot(
+                weights.astype(jnp.bfloat16), value_rows, preferred_element_type=jnp.float32
+            )
+            attended = (summed / denominator).astype(jnp.bfloat16)
             out[first:after] = attended.reshape(step, rows, width)
             scores = later
 

time: 43.6 us -> 43.5 us (level)
  no operation moved by 1% of the time
where the time goes in v4:
time: 43.5 us; the launch traced here: 43.4 us
  blocking collectives  39.9 us (92%)
  Pallas kernels  1.48 us (3%)
  other arithmetic  1.22 us (3%)
  local copies, waits for them, and re-layouts  0.76 us (2%)
    all_to_all x1, blocking collectives, whole_heads(): exchange(packed)  27.7 us
    all_to_all x1, blocking collectives, whole_heads(): returned = exchange(attended)  12.2 us
    pallas_call x1, Pallas kernels, whole_heads(): pl.pallas_call(functools.partial(head_kernel, order, min(QUERY_TILE, devi...  1.48 us
    transpose x1, other arithmetic, whole_heads(): packed.transpose(1, 0, 2)  1.22 us

profile of v4, /device:TPU:0, one launch (start us, length us, event | category | flops | bytes accessed | tf_op | source)
XLA Modules:
  0.0 43.4 jit_solution(3593120165939331717)
XLA Ops:
  0.0 1.2 %bitcast_bitcast_fusion = bf16[24,96,128]{2,1,0:T(8,128)(2,1)S(1)} fusion(bf16[32,3072]{1,0:T(8,128)(2,1)} %param.5, bf16[32,3072]{1,0:T(8,128)(2,1)} %param.4, bf16[32,3072]{1,0:T(8,128)(2,1)} %param.3), kind=kLoop, calls=%fused_computation | loop fusion | flops 1769472 | bytes 1179648 | tf_op jit(solution)/shard_map/transpose | solution.py:157
  1.2 0.1 pad.4
  1.3 27.7 %all_to_all.10.received = bf16[32,96,128]{2,1,0:T(8,128)(2,1)S(1)} all-to-all(bf16[32,96,128]{2,1,0:T(8,128)(2,1)S(1)} %pad.4), channel_id=1, replica_groups={{21,27,12,18,25,15,16,6,13,19,4,10,17,7,8,30,5,11,28,2,9,31,0,22,29,3,2..., dimensions={0} | all-to-all | bytes 1572864 | tf_op jit(solution)/shard_map/all_to_all | solution.py:162
  29.0 1.5 %shard_map.37 = bf16[32,32,128]{2,1,0:T(8,128)(2,1)S(1)} custom-call(bf16[32,96,128]{2,1,0:T(8,128)(2,1)S(1)} %all_to_all.10.received), custom_call_target="tpu_custom_call" | custom-call | tf_op jit(solution)/shard_map/pallas_call | solution.py:158
  30.5 12.2 %all_to_all.11 = bf16[32,32,128]{2,1,0:T(8,128)(2,1)S(1)} all-to-all(bf16[32,32,128]{2,1,0:T(8,128)(2,1)S(1)} %shard_map.37), channel_id=1, replica_groups={{21,27,12,18,25,15,16,6,13,19,4,10,17,7,8,30,5,11,28,2,9,31,0,22,29,3,2..., dimensions={0} | all-to-all | bytes 524288 | tf_op jit(solution)/shard_map/all_to_all | solution.py:163
  42.7 0.7 %copy_bitcast_fusion = bf16[32,3072]{1,0:T(8,128)(2,1)} fusion(bf16[32,32,128]{2,1,0:T(8,128)(2,1)S(1)} %all_to_all.11), kind=kLoop, calls=%fused_computation.2 | loop fusion | bytes 393216 | tf_op jit(solution)/shard_map/reshape | solution.py:164
